TPU v7x, 256 devices: a whole 4x4x8 slice. The times are simulated.
256 devices in a mesh: seq: 32 (over x, z), head: 8 (over y, core).
Axes of the slice: x: 4, y: 4, z: 8, core: 2. Of those that a mesh axis runs over, the one named last changes fastest.
Arguments:
- tokens: bfloat16 [8192, 2048], P(('seq', 'head')), may hold values from -6 to 6
- w_query: bfloat16 [2048, 2048], P(None, 'head'), may hold values from -0.125 to 0.125
- w_key: bfloat16 [2048, 2048], P(None, 'head'), may hold values from -1 to 1
- w_value: bfloat16 [2048, 4096], P(None, 'head'), may hold values from -0.125 to 0.125
- w_beta: bfloat16 [2048, 32], P(None, 'head'), may hold values from -0.1875 to 0.1875
- w_out: bfloat16 [4096, 2048], P('head'), may hold values from -0.09375 to 0.09375
- mask_query: int32 [32, 32], P(None, 'head'), may hold values 0 or 1
- mask_key: int32 [32, 32], P(None, 'head'), may hold values 0 or 1
- mask_value: int32 [32, 64], P(None, 'head'), may hold values 0 or 1
- mask_out: int32 [64, 32], P('head'), may hold values 0 or 1
- decay_rate: float32 [8192, 32], P('seq', 'head'), may hold values from 0.9 to 0.999999
- norm_gain: float32 [128], replicated, may hold values from 0.1 to 1.9
Outputs:
- mixed_out: bfloat16 [8192, 2048], P(('seq', 'head'))
Inputs may be any that keep to these rules, and one draw needn't show every extreme that they name: `mask_query`: 1 keeps a 64 x 64 weight block, 0 prunes it. `mask_key`: 1 keeps a 64 x 64 weight block, 0 prunes it. `mask_value`: 1 keeps a 64 x 64 weight block, 0 prunes it. `mask_out`: 1 keeps a 64 x 64 weight block, 0 prunes it.
All inputs are finite; a program needn't handle non-finite values.
Results may differ from a plain program's by a relative error of at most 0.029.
Values may be sent and summed in bfloat16 or wider, within the bound.
A program may use at most 128 MiB of HBM per device.

v0:
```python
import math

import jax
import jax.numpy as jnp
from jax import lax
from jax.sharding import PartitionSpec as P

KH = 16
VH = 32
HD = 128
BLOCK_LEN = 64
TILE = 64


def shifted(block, axis, distance):
    devices = range(lax.axis_size(axis))
    route = [(i - distance, i) for i in devices if i - distance in devices]
    return lax.ppermute(block, axis, route)


def masked(weight, mask):
    tall, broad = mask.shape
    full = jnp.broadcast_to(mask[:, None, :, None], (tall, TILE, broad, TILE)).reshape(
        tall * TILE, broad * TILE
    )
    return weight * full.astype(weight.dtype)


def unit_rows(matrix):
    return matrix * lax.rsqrt(jnp.sum(matrix * matrix, -1, keepdims=True) + 1e-06)


def projections(tokens, w_query, w_key, w_value, w_beta, mask_query, mask_key, mask_value):
    row_count = tokens.shape[0]
    raw_q = jnp.dot(tokens, masked(w_query, mask_query), preferred_element_type=jnp.float32)
    raw_k = jnp.dot(tokens, masked(w_key, mask_key), preferred_element_type=jnp.float32)
    raw_v = jnp.dot(tokens, masked(w_value, mask_value), preferred_element_type=jnp.float32)
    beta_gate = jax.nn.sigmoid(jnp.dot(tokens, w_beta, preferred_element_type=jnp.float32))
    queries = (unit_rows(raw_q.reshape(row_count, -1, HD)) * (1.0 / math.sqrt(HD))).astype(
        jnp.bfloat16
    )
    keys = unit_rows(raw_k.reshape(row_count, -1, HD)).astype(jnp.bfloat16)
    values = jax.nn.silu(raw_v.reshape(row_count, -1, HD)).astype(jnp.bfloat16)
    return (queries, keys, values, beta_gate)


def blocks(array):
    return array.reshape(array.shape[0] // BLOCK_LEN, BLOCK_LEN, array.shape[1], -1).transpose(
        0, 2, 1, 3
    )


def block_parts(query_pairs, key_pairs, keys, values, beta_gate, decay_rate):
    factor = keys.shape[-3] // key_pairs.shape[-3]
    log_decay = jnp.cumsum(jnp.log(decay_rate), axis=-1)
    spread = log_decay[..., :, None] - log_decay[..., None, :]
    positions = jnp.arange(BLOCK_LEN)
    lower_mask = positions[:, None] >= positions[None, :]
    strict_mask = positions[:, None] > positions[None, :]
    decay_ratio = jnp.where(lower_mask, jnp.exp(jnp.where(lower_mask, spread, 0.0)), 0.0)
    key_gram = jnp.repeat(
        jnp.einsum("...id,...jd->...ij", key_pairs, key_pairs, preferred_element_type=jnp.float32),
        factor,
        axis=-3,
    )
    identity = jnp.eye(BLOCK_LEN, dtype=jnp.float32)
    system = identity + jnp.where(
        strict_mask, beta_gate[..., :, None] * decay_ratio * key_gram, 0.0
    )
    right_side = jnp.concatenate(
        [(beta_gate * jnp.exp(log_decay))[..., None] * keys, beta_gate[..., None] * values], -1
    )
    solved = jax.scipy.linalg.solve_triangular(system, right_side, lower=True, unit_diagonal=True)
    key_mix = solved[..., :HD]
    value_mix = solved[..., HD:]
    pair_scores = jnp.einsum(
        "...id,...jd->...ij", query_pairs, key_pairs, preferred_element_type=jnp.float32
    )
    scores = jnp.repeat(pair_scores, factor, axis=-3) * decay_ratio
    return (log_decay, key_mix, value_mix, scores)


def block_step(carried, inputs, emit):
    highest = lax.Precision.HIGHEST
    queries, keys, log_decay, key_mix, value_mix, scores = inputs
    corrected = value_mix - jnp.einsum("hcd,hdw->hcw", key_mix, carried, precision=highest)
    last_log = log_decay[:, -1]
    tail_decay = jnp.exp(last_log[:, None] - log_decay)
    updated = jnp.exp(last_log)[:, None, None] * carried + jnp.einsum(
        "hcd,hcw->hdw", keys * tail_decay[..., None], corrected, precision=highest
    )
    if not emit:
        return (updated, None)
    emitted = jnp.exp(log_decay)[..., None] * jnp.einsum(
        "hcd,hdw->hcw", queries, carried, precision=highest
    )
    emitted = emitted + jnp.einsum("hij,hjw->hiw", scores, corrected, precision=highest)
    return (updated, emitted)


def normalize(outputs, norm_gain):
    block_count, head_count, span_len, width = outputs.shape
    flattened = outputs.transpose(0, 2, 1, 3).reshape(block_count * span_len, head_count, width)
    inv_rms = lax.rsqrt(jnp.mean(flattened * flattened, -1, keepdims=True) + 1e-06)
    return (
        (flattened * inv_rms * norm_gain)
        .astype(jnp.bfloat16)
        .reshape(block_count * span_len, head_count * width)
    )


def on_device(
    tokens,
    w_query,
    w_key,
    w_value,
    w_beta,
    w_out,
    mask_query,
    mask_key,
    mask_value,
    mask_out,
    decay_rate,
    norm_gain,
):
    highest = lax.Precision.HIGHEST
    gathered = lax.all_gather(tokens, "head", axis=0, tiled=True)
    queries, keys, values, beta_gate = projections(
        gathered, w_query, w_key, w_value, w_beta, mask_query, mask_key, mask_value
    )
    repeat_factor = VH // KH
    head_count = values.shape[1]
    query_pairs = blocks(queries)
    key_pairs = blocks(keys)
    query_blocks = blocks(jnp.repeat(queries, repeat_factor, axis=1).astype(jnp.float32))
    key_blocks = blocks(jnp.repeat(keys, repeat_factor, axis=1).astype(jnp.float32))
    value_blocks = blocks(values.astype(jnp.float32))
    beta_blocks = blocks(beta_gate[..., None])[..., 0]
    decay_blocks = blocks(decay_rate[..., None])[..., 0]
    widened = jnp.concatenate([jnp.zeros_like(value_blocks), value_blocks], -1)
    log_decay, key_mix, value_mix, scores = block_parts(
        query_pairs, key_pairs, key_blocks, widened, beta_blocks, decay_blocks
    )
    identity = jnp.broadcast_to(jnp.eye(HD, dtype=jnp.float32), (head_count, HD, HD))
    initial = jnp.concatenate([identity, jnp.zeros((head_count, HD, HD), jnp.float32)], -1)

    def first_pass(carried, inputs):
        return block_step(carried, inputs, False)

    closing, first_outputs = lax.scan(
        first_pass, initial, (query_blocks, key_blocks, log_decay, key_mix, value_mix, scores)
    )
    transition = closing[..., :HD]
    offset = closing[..., HD:]

    def hop(hop_index, incoming):
        advanced = jnp.einsum("hde,hew->hdw", transition, incoming, precision=highest) + offset
        return shifted(advanced.astype(jnp.bfloat16), "seq", 1).astype(advanced.dtype)

    start_state = lax.fori_loop(0, lax.axis_size("seq") - 1, hop, jnp.zeros_like(offset))

    def second_pass(carried, inputs):
        return block_step(carried, inputs, True)

    ending, outputs = lax.scan(
        second_pass,
        start_state,
        (query_blocks, key_blocks, log_decay, key_mix, value_mix[..., HD:], scores),
    )
    hidden = normalize(outputs, norm_gain)
    out_weight = masked(w_out, mask_out)
    return lax.psum_scatter(
        jnp.dot(hidden, out_weight, preferred_element_type=jnp.float32).astype(jnp.bfloat16),
        "head",
        scatter_dimension=0,
        tiled=True,
    )


def solution(mesh):
    return jax.shard_map(
        on_device,
        mesh=mesh,
        in_specs=(
            P(("seq", "head"), None),
            P(None, "head"),
            P(None, "head"),
            P(None, "head"),
            P(None, "head"),
            P("head", None),
            P(None, "head"),
            P(None, "head"),
            P(None, "head"),
            P("head", None),
            P("seq", "head"),
            P(),
        ),
        out_specs=P(("seq", "head"), None),
        check_vma=False,
    )
```

profile of v0, /device:TPU:1, one launch (start us, length us, event | category | flops | bytes accessed | tf_op | source)
XLA Modules:
  0.0 505.0 jit_solution(2227616598578958160)
XLA Ops:
  15.8 6.5 %convert_element_type.94 = bf16[2048,512]{1,0:T(8,128)(2,1)} reshape(bf16[32,64,8,64]{3,2,1,0:T(8,128)(2,1)} %broadcast_in_dim.89) | data formatting | bytes 4194304 | tf_op jit(solution)/shard_map/convert_element_type | solution.py:26
  26.8 6.8 %convert_element_type.104 = bf16[512,2048]{1,0:T(8,128)(2,1)} reshape(bf16[8,64,32,64]{3,2,1,0:T(8,128)(2,1)} %broadcast_in_dim.95) | data formatting | bytes 4194304 | tf_op jit(solution)/shard_map/convert_element_type | solution.py:26
  51.0 78.8 %custom-call.4 = f32[4,4,1,64,64]{3,4,2,1,0:T(8,128)S(1)} custom-call(f32[4,4,1,64,64]{4,3,2,1,0:T(8,128)S(1)} %select_add_fusion), custom_call_target="InvertDiagBlocksLowerTriangular" | custom-call | tf_op jit(solution)/shard_map/jit(_solve_triangular)/vmap(vmap())/triangular_solve | solution.py:73
  138.7 11.2 %while.33 = (s32[]{:T(128)}, f32[4,128,256]{2,1,0:T(8,128)S(1)}, f32[4,4,64]{2,1,0:T(4,128)}, f32[4,4,64,128]{3,2,1,0:T(8,128)S(1)}, f32[4,4,64,256]{3,2,1,0:T(8...) while((s32[]{:T(128)}, f32[4,128,256]{2,1,0:T(8,128)S(1)}, f32[4,4,64]{2,1,0:T(4,128)}, ...), condition=%wide.region_3.4_spmd, body=%wide.region_2.3_spmd.sunk | while | flops 201687296 | bytes 2629289 | solution.py:150
  152.2 240.7 %while.35 = (s32[]{:T(128)}, f32[4,128,128]{2,1,0:T(8,128)S(1)}, f32[4,128,128]{2,1,0:T(8,128)S(1)}, f32[4,128,128]{2,1,0:T(8,128)S(1)}, s32[]{:T(128)}, /*index=5*/s32[]{:T(128)}) while((s32[]{:T(128)}, f32[4,128,128]{2,1,0:T(8,128)S(1)}, f32[4,128,128]{2,1,0:T(8,128)S(1)}, f32[4,128,128]{2,1,0:T(8,128)S(1)}, s32[]{:T(128)}, ...), condition=%wide.region_5.6_spmd.clone, body=%wide.region_4.5_spmd.clone.sunk | while | flops 100925440 | bytes 1835127 | solution.py:160
  184.5 5.0 collective-permute-start
  191.8 5.0 collective-permute-start
  199.2 5.0 collective-permute-start
  207.0 5.3 %collective-permute-start = (bf16[4,128,128]{2,1,0:T(8,128)(2,1)S(1)}, bf16[4,128,128]{2,1,0:T(8,128)(2,1)S(1)}, u32[]{:S(2)}, u32[]{:S(2)}) collective-permute-start(bf16[4,128,128]{2,1,0:T(8,128)(2,1)S(1)} %fusion.110), channel_id=1, source_target_pairs={{0,8},{8,16},{16,24},{24,32},{32,40},{40,48},{48,56},{56,64},{64,7... | collective-permute-start | bytes 393224 | tf_op jit(solution)/shard_map/while/body/eval_jaxpr/ppermute | solution.py:18
  215.8 5.1 %collective-permute-start = (bf16[4,128,128]{2,1,0:T(8,128)(2,1)S(1)}, bf16[4,128,128]{2,1,0:T(8,128)(2,1)S(1)}, u32[]{:S(2)}, u32[]{:S(2)}) collective-permute-start(bf16[4,128,128]{2,1,0:T(8,128)(2,1)S(1)} %fusion.110), channel_id=1, source_target_pairs={{0,8},{8,16},{16,24},{24,32},{32,40},{40,48},{48,56},{56,64},{64,7... | collective-permute-start | bytes 393224 | tf_op jit(solution)/shard_map/while/body/eval_jaxpr/ppermute | solution.py:18
  223.3 5.2 %collective-permute-start = (bf16[4,128,128]{2,1,0:T(8,128)(2,1)S(1)}, bf16[4,128,128]{2,1,0:T(8,128)(2,1)S(1)}, u32[]{:S(2)}, u32[]{:S(2)}) collective-permute-start(bf16[4,128,128]{2,1,0:T(8,128)(2,1)S(1)} %fusion.110), channel_id=1, source_target_pairs={{0,8},{8,16},{16,24},{24,32},{32,40},{40,48},{48,56},{56,64},{64,7... | collective-permute-start | bytes 393224 | tf_op jit(solution)/shard_map/while/body/eval_jaxpr/ppermute | solution.py:18
  230.9 4.9 collective-permute-start
  238.1 5.3 %collective-permute-start = (bf16[4,128,128]{2,1,0:T(8,128)(2,1)S(1)}, bf16[4,128,128]{2,1,0:T(8,128)(2,1)S(1)}, u32[]{:S(2)}, u32[]{:S(2)}) collective-permute-start(bf16[4,128,128]{2,1,0:T(8,128)(2,1)S(1)} %fusion.110), channel_id=1, source_target_pairs={{0,8},{8,16},{16,24},{24,32},{32,40},{40,48},{48,56},{56,64},{64,7... | collective-permute-start | bytes 393224 | tf_op jit(solution)/shard_map/while/body/eval_jaxpr/ppermute | solution.py:18
  245.8 5.0 collective-permute-start
  253.2 5.0 collective-permute-start
  260.6 5.0 collective-permute-start
  268.5 5.3 %collective-permute-start = (bf16[4,128,128]{2,1,0:T(8,128)(2,1)S(1)}, bf16[4,128,128]{2,1,0:T(8,128)(2,1)S(1)}, u32[]{:S(2)}, u32[]{:S(2)}) collective-permute-start(bf16[4,128,128]{2,1,0:T(8,128)(2,1)S(1)} %fusion.110), channel_id=1, source_target_pairs={{0,8},{8,16},{16,24},{24,32},{32,40},{40,48},{48,56},{56,64},{64,7... | collective-permute-start | bytes 393224 | tf_op jit(solution)/shard_map/while/body/eval_jaxpr/ppermute | solution.py:18
  277.2 5.3 %collective-permute-start = (bf16[4,128,128]{2,1,0:T(8,128)(2,1)S(1)}, bf16[4,128,128]{2,1,0:T(8,128)(2,1)S(1)}, u32[]{:S(2)}, u32[]{:S(2)}) collective-permute-start(bf16[4,128,128]{2,1,0:T(8,128)(2,1)S(1)} %fusion.110), channel_id=1, source_target_pairs={{0,8},{8,16},{16,24},{24,32},{32,40},{40,48},{48,56},{56,64},{64,7... | collective-permute-start | bytes 393224 | tf_op jit(solution)/shard_map/while/body/eval_jaxpr/ppermute | solution.py:18
  292.1 5.3 %collective-permute-start = (bf16[4,128,128]{2,1,0:T(8,128)(2,1)S(1)}, bf16[4,128,128]{2,1,0:T(8,128)(2,1)S(1)}, u32[]{:S(2)}, u32[]{:S(2)}) collective-permute-start(bf16[4,128,128]{2,1,0:T(8,128)(2,1)S(1)} %fusion.110), channel_id=1, source_target_pairs={{0,8},{8,16},{16,24},{24,32},{32,40},{40,48},{48,56},{56,64},{64,7... | collective-permute-start | bytes 393224 | tf_op jit(solution)/shard_map/while/body/eval_jaxpr/ppermute | solution.py:18
  299.8 5.3 %collective-permute-start = (bf16[4,128,128]{2,1,0:T(8,128)(2,1)S(1)}, bf16[4,128,128]{2,1,0:T(8,128)(2,1)S(1)}, u32[]{:S(2)}, u32[]{:S(2)}) collective-permute-start(bf16[4,128,128]{2,1,0:T(8,128)(2,1)S(1)} %fusion.110), channel_id=1, source_target_pairs={{0,8},{8,16},{16,24},{24,32},{32,40},{40,48},{48,56},{56,64},{64,7... | collective-permute-start | bytes 393224 | tf_op jit(solution)/shard_map/while/body/eval_jaxpr/ppermute | solution.py:18
  307.5 5.4 %collective-permute-start = (bf16[4,128,128]{2,1,0:T(8,128)(2,1)S(1)}, bf16[4,128,128]{2,1,0:T(8,128)(2,1)S(1)}, u32[]{:S(2)}, u32[]{:S(2)}) collective-permute-start(bf16[4,128,128]{2,1,0:T(8,128)(2,1)S(1)} %fusion.110), channel_id=1, source_target_pairs={{0,8},{8,16},{16,24},{24,32},{32,40},{40,48},{48,56},{56,64},{64,7... | collective-permute-start | bytes 393224 | tf_op jit(solution)/shard_map/while/body/eval_jaxpr/ppermute | solution.py:18
  315.3 7.3 %collective-permute-start = (bf16[4,128,128]{2,1,0:T(8,128)(2,1)S(1)}, bf16[4,128,128]{2,1,0:T(8,128)(2,1)S(1)}, u32[]{:S(2)}, u32[]{:S(2)}) collective-permute-start(bf16[4,128,128]{2,1,0:T(8,128)(2,1)S(1)} %fusion.110), channel_id=1, source_target_pairs={{0,8},{8,16},{16,24},{24,32},{32,40},{40,48},{48,56},{56,64},{64,7... | collective-permute-start | bytes 393224 | tf_op jit(solution)/shard_map/while/body/eval_jaxpr/ppermute | solution.py:18
  325.0 5.5 %collective-permute-start = (bf16[4,128,128]{2,1,0:T(8,128)(2,1)S(1)}, bf16[4,128,128]{2,1,0:T(8,128)(2,1)S(1)}, u32[]{:S(2)}, u32[]{:S(2)}) collective-permute-start(bf16[4,128,128]{2,1,0:T(8,128)(2,1)S(1)} %fusion.110), channel_id=1, source_target_pairs={{0,8},{8,16},{16,24},{24,32},{32,40},{40,48},{48,56},{56,64},{64,7... | collective-permute-start | bytes 393224 | tf_op jit(solution)/shard_map/while/body/eval_jaxpr/ppermute | solution.py:18
  332.8 5.5 %collective-permute-start = (bf16[4,128,128]{2,1,0:T(8,128)(2,1)S(1)}, bf16[4,128,128]{2,1,0:T(8,128)(2,1)S(1)}, u32[]{:S(2)}, u32[]{:S(2)}) collective-permute-start(bf16[4,128,128]{2,1,0:T(8,128)(2,1)S(1)} %fusion.110), channel_id=1, source_target_pairs={{0,8},{8,16},{16,24},{24,32},{32,40},{40,48},{48,56},{56,64},{64,7... | collective-permute-start | bytes 393224 | tf_op jit(solution)/shard_map/while/body/eval_jaxpr/ppermute | solution.py:18
  340.7 6.2 %collective-permute-start = (bf16[4,128,128]{2,1,0:T(8,128)(2,1)S(1)}, bf16[4,128,128]{2,1,0:T(8,128)(2,1)S(1)}, u32[]{:S(2)}, u32[]{:S(2)}) collective-permute-start(bf16[4,128,128]{2,1,0:T(8,128)(2,1)S(1)} %fusion.110), channel_id=1, source_target_pairs={{0,8},{8,16},{16,24},{24,32},{32,40},{40,48},{48,56},{56,64},{64,7... | collective-permute-start | bytes 393224 | tf_op jit(solution)/shard_map/while/body/eval_jaxpr/ppermute | solution.py:18
  349.3 6.2 %collective-permute-start = (bf16[4,128,128]{2,1,0:T(8,128)(2,1)S(1)}, bf16[4,128,128]{2,1,0:T(8,128)(2,1)S(1)}, u32[]{:S(2)}, u32[]{:S(2)}) collective-permute-start(bf16[4,128,128]{2,1,0:T(8,128)(2,1)S(1)} %fusion.110), channel_id=1, source_target_pairs={{0,8},{8,16},{16,24},{24,32},{32,40},{40,48},{48,56},{56,64},{64,7... | collective-permute-start | bytes 393224 | tf_op jit(solution)/shard_map/while/body/eval_jaxpr/ppermute | solution.py:18
  358.0 6.2 %collective-permute-start = (bf16[4,128,128]{2,1,0:T(8,128)(2,1)S(1)}, bf16[4,128,128]{2,1,0:T(8,128)(2,1)S(1)}, u32[]{:S(2)}, u32[]{:S(2)}) collective-permute-start(bf16[4,128,128]{2,1,0:T(8,128)(2,1)S(1)} %fusion.110), channel_id=1, source_target_pairs={{0,8},{8,16},{16,24},{24,32},{32,40},{40,48},{48,56},{56,64},{64,7... | collective-permute-start | bytes 393224 | tf_op jit(solution)/shard_map/while/body/eval_jaxpr/ppermute | solution.py:18
  368.0 5.9 %collective-permute-start = (bf16[4,128,128]{2,1,0:T(8,128)(2,1)S(1)}, bf16[4,128,128]{2,1,0:T(8,128)(2,1)S(1)}, u32[]{:S(2)}, u32[]{:S(2)}) collective-permute-start(bf16[4,128,128]{2,1,0:T(8,128)(2,1)S(1)} %fusion.110), channel_id=1, source_target_pairs={{0,8},{8,16},{16,24},{24,32},{32,40},{40,48},{48,56},{56,64},{64,7... | collective-permute-start | bytes 393224 | tf_op jit(solution)/shard_map/while/body/eval_jaxpr/ppermute | solution.py:18
  376.4 5.9 %collective-permute-start = (bf16[4,128,128]{2,1,0:T(8,128)(2,1)S(1)}, bf16[4,128,128]{2,1,0:T(8,128)(2,1)S(1)}, u32[]{:S(2)}, u32[]{:S(2)}) collective-permute-start(bf16[4,128,128]{2,1,0:T(8,128)(2,1)S(1)} %fusion.110), channel_id=1, source_target_pairs={{0,8},{8,16},{16,24},{24,32},{32,40},{40,48},{48,56},{56,64},{64,7... | collective-permute-start | bytes 393224 | tf_op jit(solution)/shard_map/while/body/eval_jaxpr/ppermute | solution.py:18
  384.7 6.3 %collective-permute-start = (bf16[4,128,128]{2,1,0:T(8,128)(2,1)S(1)}, bf16[4,128,128]{2,1,0:T(8,128)(2,1)S(1)}, u32[]{:S(2)}, u32[]{:S(2)}) collective-permute-start(bf16[4,128,128]{2,1,0:T(8,128)(2,1)S(1)} %fusion.110), channel_id=1, source_target_pairs={{0,8},{8,16},{16,24},{24,32},{32,40},{40,48},{48,56},{56,64},{64,7... | collective-permute-start | bytes 393224 | tf_op jit(solution)/shard_map/while/body/eval_jaxpr/ppermute | solution.py:18
  393.9 14.3 %while.34 = (s32[]{:T(128)}, f32[4,128,128]{2,1,0:T(8,128)S(1)}, f32[4,4,64,128]{3,2,1,0:T(8,128)S(1)}, f32[4,4,64]{2,1,0:T(4,128)}, f32[4,4,64,128]{3,2,1,0:T(8...) while((s32[]{:T(128)}, f32[4,128,128]{2,1,0:T(8,128)S(1)}, ...), condition=%wide.region_8.9_spmd, body=%wide.region_7.8_spmd.sunk | while | flops 176423168 | bytes 2502337 | solution.py:165
  413.1 85.0 %reduce-scatter.2.cloned.1.call-done = bf16[32,2048]{1,0:T(8,128)(2,1)} async-done(((bf16[256,2048]{1,0:T(8,128)(2,1)}), bf16[32,2048]{1,0:T(8,128)(2,1)}) %reduce-scatter.2.cloned.1.call-update) | async-done | bytes 131088 | tf_op jit(solution)/shard_map/reduce_scatter | solution.py:172
  (285 shorter events, 174.9 us)
Async XLA Ops:
  6.5 32.9 %all-gather.2.cloned.1.call-start = ((), (), s32[]{:S(2)}) async-start(), calls=%async_computation.1 | async-start | bytes 1179648 | tf_op jit(solution)/shard_map/all_gather | solution.py:127
  7.3 490.9 %reduce-scatter.2.cloned.1.call-start = ((), (), s32[]{:S(2)}) async-start(), calls=%async_computation.2 | async-start | bytes 1179648 | tf_op jit(solution)/shard_map/reduce_scatter | solution.py:172
  152.6 5.8 %collective-permute-start = (bf16[4,128,128]{2,1,0:T(8,128)(2,1)S(1)}, bf16[4,128,128]{2,1,0:T(8,128)(2,1)S(1)}, u32[]{:S(2)}, u32[]{:S(2)}) collective-permute-start(bf16[4,128,128]{2,1,0:T(8,128)(2,1)S(1)} %fusion.110), channel_id=1, source_target_pairs={{0,8},{8,16},{16,24},{24,32},{32,40},{40,48},{48,56},{56,64},{64,7... | collective-permute-start | bytes 393224 | tf_op jit(solution)/shard_map/while/body/eval_jaxpr/ppermute | solution.py:18
  158.9 6.0 %collective-permute-start = (bf16[4,128,128]{2,1,0:T(8,128)(2,1)S(1)}, bf16[4,128,128]{2,1,0:T(8,128)(2,1)S(1)}, u32[]{:S(2)}, u32[]{:S(2)}) collective-permute-start(bf16[4,128,128]{2,1,0:T(8,128)(2,1)S(1)} %fusion.110), channel_id=1, source_target_pairs={{0,8},{8,16},{16,24},{24,32},{32,40},{40,48},{48,56},{56,64},{64,7... | collective-permute-start | bytes 393224 | tf_op jit(solution)/shard_map/while/body/eval_jaxpr/ppermute | solution.py:18
  165.4 5.7 %collective-permute-start = (bf16[4,128,128]{2,1,0:T(8,128)(2,1)S(1)}, bf16[4,128,128]{2,1,0:T(8,128)(2,1)S(1)}, u32[]{:S(2)}, u32[]{:S(2)}) collective-permute-start(bf16[4,128,128]{2,1,0:T(8,128)(2,1)S(1)} %fusion.110), channel_id=1, source_target_pairs={{0,8},{8,16},{16,24},{24,32},{32,40},{40,48},{48,56},{56,64},{64,7... | collective-permute-start | bytes 393224 | tf_op jit(solution)/shard_map/while/body/eval_jaxpr/ppermute | solution.py:18
  177.7 6.3 %collective-permute-start = (bf16[4,128,128]{2,1,0:T(8,128)(2,1)S(1)}, bf16[4,128,128]{2,1,0:T(8,128)(2,1)S(1)}, u32[]{:S(2)}, u32[]{:S(2)}) collective-permute-start(bf16[4,128,128]{2,1,0:T(8,128)(2,1)S(1)} %fusion.110), channel_id=1, source_target_pairs={{0,8},{8,16},{16,24},{24,32},{32,40},{40,48},{48,56},{56,64},{64,7... | collective-permute-start | bytes 393224 | tf_op jit(solution)/shard_map/while/body/eval_jaxpr/ppermute | solution.py:18
  184.5 6.9 %collective-permute-start = (bf16[4,128,128]{2,1,0:T(8,128)(2,1)S(1)}, bf16[4,128,128]{2,1,0:T(8,128)(2,1)S(1)}, u32[]{:S(2)}, u32[]{:S(2)}) collective-permute-start(bf16[4,128,128]{2,1,0:T(8,128)(2,1)S(1)} %fusion.110), channel_id=1, source_target_pairs={{0,8},{8,16},{16,24},{24,32},{32,40},{40,48},{48,56},{56,64},{64,7... | collective-permute-start | bytes 393224 | tf_op jit(solution)/shard_map/while/body/eval_jaxpr/ppermute | solution.py:18
  191.8 6.9 %collective-permute-start = (bf16[4,128,128]{2,1,0:T(8,128)(2,1)S(1)}, bf16[4,128,128]{2,1,0:T(8,128)(2,1)S(1)}, u32[]{:S(2)}, u32[]{:S(2)}) collective-permute-start(bf16[4,128,128]{2,1,0:T(8,128)(2,1)S(1)} %fusion.110), channel_id=1, source_target_pairs={{0,8},{8,16},{16,24},{24,32},{32,40},{40,48},{48,56},{56,64},{64,7... | collective-permute-start | bytes 393224 | tf_op jit(solution)/shard_map/while/body/eval_jaxpr/ppermute | solution.py:18
  199.2 7.3 %collective-permute-start = (bf16[4,128,128]{2,1,0:T(8,128)(2,1)S(1)}, bf16[4,128,128]{2,1,0:T(8,128)(2,1)S(1)}, u32[]{:S(2)}, u32[]{:S(2)}) collective-permute-start(bf16[4,128,128]{2,1,0:T(8,128)(2,1)S(1)} %fusion.110), channel_id=1, source_target_pairs={{0,8},{8,16},{16,24},{24,32},{32,40},{40,48},{48,56},{56,64},{64,7... | collective-permute-start | bytes 393224 | tf_op jit(solution)/shard_map/while/body/eval_jaxpr/ppermute | solution.py:18
  207.0 8.4 %collective-permute-start = (bf16[4,128,128]{2,1,0:T(8,128)(2,1)S(1)}, bf16[4,128,128]{2,1,0:T(8,128)(2,1)S(1)}, u32[]{:S(2)}, u32[]{:S(2)}) collective-permute-start(bf16[4,128,128]{2,1,0:T(8,128)(2,1)S(1)} %fusion.110), channel_id=1, source_target_pairs={{0,8},{8,16},{16,24},{24,32},{32,40},{40,48},{48,56},{56,64},{64,7... | collective-permute-start | bytes 393224 | tf_op jit(solution)/shard_map/while/body/eval_jaxpr/ppermute | solution.py:18
  215.8 7.1 %collective-permute-start = (bf16[4,128,128]{2,1,0:T(8,128)(2,1)S(1)}, bf16[4,128,128]{2,1,0:T(8,128)(2,1)S(1)}, u32[]{:S(2)}, u32[]{:S(2)}) collective-permute-start(bf16[4,128,128]{2,1,0:T(8,128)(2,1)S(1)} %fusion.110), channel_id=1, source_target_pairs={{0,8},{8,16},{16,24},{24,32},{32,40},{40,48},{48,56},{56,64},{64,7... | collective-permute-start | bytes 393224 | tf_op jit(solution)/shard_map/while/body/eval_jaxpr/ppermute | solution.py:18
  223.3 7.1 %collective-permute-start = (bf16[4,128,128]{2,1,0:T(8,128)(2,1)S(1)}, bf16[4,128,128]{2,1,0:T(8,128)(2,1)S(1)}, u32[]{:S(2)}, u32[]{:S(2)}) collective-permute-start(bf16[4,128,128]{2,1,0:T(8,128)(2,1)S(1)} %fusion.110), channel_id=1, source_target_pairs={{0,8},{8,16},{16,24},{24,32},{32,40},{40,48},{48,56},{56,64},{64,7... | collective-permute-start | bytes 393224 | tf_op jit(solution)/shard_map/while/body/eval_jaxpr/ppermute | solution.py:18
  230.9 6.8 %collective-permute-start = (bf16[4,128,128]{2,1,0:T(8,128)(2,1)S(1)}, bf16[4,128,128]{2,1,0:T(8,128)(2,1)S(1)}, u32[]{:S(2)}, u32[]{:S(2)}) collective-permute-start(bf16[4,128,128]{2,1,0:T(8,128)(2,1)S(1)} %fusion.110), channel_id=1, source_target_pairs={{0,8},{8,16},{16,24},{24,32},{32,40},{40,48},{48,56},{56,64},{64,7... | collective-permute-start | bytes 393224 | tf_op jit(solution)/shard_map/while/body/eval_jaxpr/ppermute | solution.py:18
  238.1 7.3 %collective-permute-start = (bf16[4,128,128]{2,1,0:T(8,128)(2,1)S(1)}, bf16[4,128,128]{2,1,0:T(8,128)(2,1)S(1)}, u32[]{:S(2)}, u32[]{:S(2)}) collective-permute-start(bf16[4,128,128]{2,1,0:T(8,128)(2,1)S(1)} %fusion.110), channel_id=1, source_target_pairs={{0,8},{8,16},{16,24},{24,32},{32,40},{40,48},{48,56},{56,64},{64,7... | collective-permute-start | bytes 393224 | tf_op jit(solution)/shard_map/while/body/eval_jaxpr/ppermute | solution.py:18
  245.8 6.9 %collective-permute-start = (bf16[4,128,128]{2,1,0:T(8,128)(2,1)S(1)}, bf16[4,128,128]{2,1,0:T(8,128)(2,1)S(1)}, u32[]{:S(2)}, u32[]{:S(2)}) collective-permute-start(bf16[4,128,128]{2,1,0:T(8,128)(2,1)S(1)} %fusion.110), channel_id=1, source_target_pairs={{0,8},{8,16},{16,24},{24,32},{32,40},{40,48},{48,56},{56,64},{64,7... | collective-permute-start | bytes 393224 | tf_op jit(solution)/shard_map/while/body/eval_jaxpr/ppermute | solution.py:18
  253.2 6.9 %collective-permute-start = (bf16[4,128,128]{2,1,0:T(8,128)(2,1)S(1)}, bf16[4,128,128]{2,1,0:T(8,128)(2,1)S(1)}, u32[]{:S(2)}, u32[]{:S(2)}) collective-permute-start(bf16[4,128,128]{2,1,0:T(8,128)(2,1)S(1)} %fusion.110), channel_id=1, source_target_pairs={{0,8},{8,16},{16,24},{24,32},{32,40},{40,48},{48,56},{56,64},{64,7... | collective-permute-start | bytes 393224 | tf_op jit(solution)/shard_map/while/body/eval_jaxpr/ppermute | solution.py:18
  260.6 7.5 %collective-permute-start = (bf16[4,128,128]{2,1,0:T(8,128)(2,1)S(1)}, bf16[4,128,128]{2,1,0:T(8,128)(2,1)S(1)}, u32[]{:S(2)}, u32[]{:S(2)}) collective-permute-start(bf16[4,128,128]{2,1,0:T(8,128)(2,1)S(1)} %fusion.110), channel_id=1, source_target_pairs={{0,8},{8,16},{16,24},{24,32},{32,40},{40,48},{48,56},{56,64},{64,7... | collective-permute-start | bytes 393224 | tf_op jit(solution)/shard_map/while/body/eval_jaxpr/ppermute | solution.py:18
  268.5 8.3 %collective-permute-start = (bf16[4,128,128]{2,1,0:T(8,128)(2,1)S(1)}, bf16[4,128,128]{2,1,0:T(8,128)(2,1)S(1)}, u32[]{:S(2)}, u32[]{:S(2)}) collective-permute-start(bf16[4,128,128]{2,1,0:T(8,128)(2,1)S(1)} %fusion.110), channel_id=1, source_target_pairs={{0,8},{8,16},{16,24},{24,32},{32,40},{40,48},{48,56},{56,64},{64,7... | collective-permute-start | bytes 393224 | tf_op jit(solution)/shard_map/while/body/eval_jaxpr/ppermute | solution.py:18
  277.2 7.2 %collective-permute-start = (bf16[4,128,128]{2,1,0:T(8,128)(2,1)S(1)}, bf16[4,128,128]{2,1,0:T(8,128)(2,1)S(1)}, u32[]{:S(2)}, u32[]{:S(2)}) collective-permute-start(bf16[4,128,128]{2,1,0:T(8,128)(2,1)S(1)} %fusion.110), channel_id=1, source_target_pairs={{0,8},{8,16},{16,24},{24,32},{32,40},{40,48},{48,56},{56,64},{64,7... | collective-permute-start | bytes 393224 | tf_op jit(solution)/shard_map/while/body/eval_jaxpr/ppermute | solution.py:18
  284.9 6.8 %collective-permute-start = (bf16[4,128,128]{2,1,0:T(8,128)(2,1)S(1)}, bf16[4,128,128]{2,1,0:T(8,128)(2,1)S(1)}, u32[]{:S(2)}, u32[]{:S(2)}) collective-permute-start(bf16[4,128,128]{2,1,0:T(8,128)(2,1)S(1)} %fusion.110), channel_id=1, source_target_pairs={{0,8},{8,16},{16,24},{24,32},{32,40},{40,48},{48,56},{56,64},{64,7... | collective-permute-start | bytes 393224 | tf_op jit(solution)/shard_map/while/body/eval_jaxpr/ppermute | solution.py:18
  292.1 7.3 %collective-permute-start = (bf16[4,128,128]{2,1,0:T(8,128)(2,1)S(1)}, bf16[4,128,128]{2,1,0:T(8,128)(2,1)S(1)}, u32[]{:S(2)}, u32[]{:S(2)}) collective-permute-start(bf16[4,128,128]{2,1,0:T(8,128)(2,1)S(1)} %fusion.110), channel_id=1, source_target_pairs={{0,8},{8,16},{16,24},{24,32},{32,40},{40,48},{48,56},{56,64},{64,7... | collective-permute-start | bytes 393224 | tf_op jit(solution)/shard_map/while/body/eval_jaxpr/ppermute | solution.py:18
  299.8 7.3 %collective-permute-start = (bf16[4,128,128]{2,1,0:T(8,128)(2,1)S(1)}, bf16[4,128,128]{2,1,0:T(8,128)(2,1)S(1)}, u32[]{:S(2)}, u32[]{:S(2)}) collective-permute-start(bf16[4,128,128]{2,1,0:T(8,128)(2,1)S(1)} %fusion.110), channel_id=1, source_target_pairs={{0,8},{8,16},{16,24},{24,32},{32,40},{40,48},{48,56},{56,64},{64,7... | collective-permute-start | bytes 393224 | tf_op jit(solution)/shard_map/while/body/eval_jaxpr/ppermute | solution.py:18
  307.5 7.4 %collective-permute-start = (bf16[4,128,128]{2,1,0:T(8,128)(2,1)S(1)}, bf16[4,128,128]{2,1,0:T(8,128)(2,1)S(1)}, u32[]{:S(2)}, u32[]{:S(2)}) collective-permute-start(bf16[4,128,128]{2,1,0:T(8,128)(2,1)S(1)} %fusion.110), channel_id=1, source_target_pairs={{0,8},{8,16},{16,24},{24,32},{32,40},{40,48},{48,56},{56,64},{64,7... | collective-permute-start | bytes 393224 | tf_op jit(solution)/shard_map/while/body/eval_jaxpr/ppermute | solution.py:18
  315.3 9.2 %collective-permute-start = (bf16[4,128,128]{2,1,0:T(8,128)(2,1)S(1)}, bf16[4,128,128]{2,1,0:T(8,128)(2,1)S(1)}, u32[]{:S(2)}, u32[]{:S(2)}) collective-permute-start(bf16[4,128,128]{2,1,0:T(8,128)(2,1)S(1)} %fusion.110), channel_id=1, source_target_pairs={{0,8},{8,16},{16,24},{24,32},{32,40},{40,48},{48,56},{56,64},{64,7... | collective-permute-start | bytes 393224 | tf_op jit(solution)/shard_map/while/body/eval_jaxpr/ppermute | solution.py:18
  325.0 7.4 %collective-permute-start = (bf16[4,128,128]{2,1,0:T(8,128)(2,1)S(1)}, bf16[4,128,128]{2,1,0:T(8,128)(2,1)S(1)}, u32[]{:S(2)}, u32[]{:S(2)}) collective-permute-start(bf16[4,128,128]{2,1,0:T(8,128)(2,1)S(1)} %fusion.110), channel_id=1, source_target_pairs={{0,8},{8,16},{16,24},{24,32},{32,40},{40,48},{48,56},{56,64},{64,7... | collective-permute-start | bytes 393224 | tf_op jit(solution)/shard_map/while/body/eval_jaxpr/ppermute | solution.py:18
  332.8 7.4 %collective-permute-start = (bf16[4,128,128]{2,1,0:T(8,128)(2,1)S(1)}, bf16[4,128,128]{2,1,0:T(8,128)(2,1)S(1)}, u32[]{:S(2)}, u32[]{:S(2)}) collective-permute-start(bf16[4,128,128]{2,1,0:T(8,128)(2,1)S(1)} %fusion.110), channel_id=1, source_target_pairs={{0,8},{8,16},{16,24},{24,32},{32,40},{40,48},{48,56},{56,64},{64,7... | collective-permute-start | bytes 393224 | tf_op jit(solution)/shard_map/while/body/eval_jaxpr/ppermute | solution.py:18
  340.7 8.2 %collective-permute-start = (bf16[4,128,128]{2,1,0:T(8,128)(2,1)S(1)}, bf16[4,128,128]{2,1,0:T(8,128)(2,1)S(1)}, u32[]{:S(2)}, u32[]{:S(2)}) collective-permute-start(bf16[4,128,128]{2,1,0:T(8,128)(2,1)S(1)} %fusion.110), channel_id=1, source_target_pairs={{0,8},{8,16},{16,24},{24,32},{32,40},{40,48},{48,56},{56,64},{64,7... | collective-permute-start | bytes 393224 | tf_op jit(solution)/shard_map/while/body/eval_jaxpr/ppermute | solution.py:18
  349.3 8.3 %collective-permute-start = (bf16[4,128,128]{2,1,0:T(8,128)(2,1)S(1)}, bf16[4,128,128]{2,1,0:T(8,128)(2,1)S(1)}, u32[]{:S(2)}, u32[]{:S(2)}) collective-permute-start(bf16[4,128,128]{2,1,0:T(8,128)(2,1)S(1)} %fusion.110), channel_id=1, source_target_pairs={{0,8},{8,16},{16,24},{24,32},{32,40},{40,48},{48,56},{56,64},{64,7... | collective-permute-start | bytes 393224 | tf_op jit(solution)/shard_map/while/body/eval_jaxpr/ppermute | solution.py:18
  358.0 9.5 %collective-permute-start = (bf16[4,128,128]{2,1,0:T(8,128)(2,1)S(1)}, bf16[4,128,128]{2,1,0:T(8,128)(2,1)S(1)}, u32[]{:S(2)}, u32[]{:S(2)}) collective-permute-start(bf16[4,128,128]{2,1,0:T(8,128)(2,1)S(1)} %fusion.110), channel_id=1, source_target_pairs={{0,8},{8,16},{16,24},{24,32},{32,40},{40,48},{48,56},{56,64},{64,7... | collective-permute-start | bytes 393224 | tf_op jit(solution)/shard_map/while/body/eval_jaxpr/ppermute | solution.py:18
  368.0 8.0 %collective-permute-start = (bf16[4,128,128]{2,1,0:T(8,128)(2,1)S(1)}, bf16[4,128,128]{2,1,0:T(8,128)(2,1)S(1)}, u32[]{:S(2)}, u32[]{:S(2)}) collective-permute-start(bf16[4,128,128]{2,1,0:T(8,128)(2,1)S(1)} %fusion.110), channel_id=1, source_target_pairs={{0,8},{8,16},{16,24},{24,32},{32,40},{40,48},{48,56},{56,64},{64,7... | collective-permute-start | bytes 393224 | tf_op jit(solution)/shard_map/while/body/eval_jaxpr/ppermute | solution.py:18
  376.4 7.8 %collective-permute-start = (bf16[4,128,128]{2,1,0:T(8,128)(2,1)S(1)}, bf16[4,128,128]{2,1,0:T(8,128)(2,1)S(1)}, u32[]{:S(2)}, u32[]{:S(2)}) collective-permute-start(bf16[4,128,128]{2,1,0:T(8,128)(2,1)S(1)} %fusion.110), channel_id=1, source_target_pairs={{0,8},{8,16},{16,24},{24,32},{32,40},{40,48},{48,56},{56,64},{64,7... | collective-permute-start | bytes 393224 | tf_op jit(solution)/shard_map/while/body/eval_jaxpr/ppermute | solution.py:18
  384.7 8.2 %collective-permute-start = (bf16[4,128,128]{2,1,0:T(8,128)(2,1)S(1)}, bf16[4,128,128]{2,1,0:T(8,128)(2,1)S(1)}, u32[]{:S(2)}, u32[]{:S(2)}) collective-permute-start(bf16[4,128,128]{2,1,0:T(8,128)(2,1)S(1)} %fusion.110), channel_id=1, source_target_pairs={{0,8},{8,16},{16,24},{24,32},{32,40},{40,48},{48,56},{56,64},{64,7... | collective-permute-start | bytes 393224 | tf_op jit(solution)/shard_map/while/body/eval_jaxpr/ppermute | solution.py:18
  (28 other events, 441.7 us)
Sparse Core Ops, SparseCore 0:
  9.2 30.1 all-gather.1
  413.3 84.8 reduce-scatter.1
where the time goes:
time: 508 us; the launch traced here: 505 us
  starting transfers between devices  162 us (32%)
  waiting for transfers between devices  154 us (30%)
  other arithmetic  92.7 us (18%)
  matrix products  41.5 us (8%)
  local copies, waits for them, and re-layouts  39.4 us (8%)
  between operations  14 us (3%)
    ppermute x31, starting transfers between devices, shifted(): return lax.ppermute(block, axis, route)  162 us
    reduce_scatter x1, waiting for transfers between devices, on_device(): lax.psum_scatter(jnp.dot(hidden, out_weight, preferred_element_type=jnp.f...  85 us
    another operation x5, other arithmetic, block_parts(): jax.scipy.linalg.solve_triangular(system, right_side, lower=True, unit_di...  80.5 us
    ppermute x31, waiting for transfers between devices, shifted(): return lax.ppermute(block, axis, route)  65.2 us
    convert_element_type x7, local copies, waits for them, and re-layouts, masked(): return weight * full.astype(weight.dtype)  17.1 us
    dot_general x31, matrix products, hop(): jnp.einsum('hde,hew->hdw', transition, incoming, precision=highest) + offset  12.2 us
  transfers between devices with their start and end apart: 33, of which 33 were waited for; matrix products, arithmetic and copies ran while one was open for 6% of the time, Pallas kernels for 0%

commit v1 on v0

v1 whole, which is shorter than its diff:
```python
import functools
import math

import jax
import jax.numpy as jnp
from jax import lax
from jax.experimental import pallas as pl
from jax.experimental.pallas import tpu as pltpu
from jax.sharding import PartitionSpec as P

HD = 128
TILE = 64
RING = 8
CORES = 2
MESH = pl.DeviceIdType.MESH
F32 = jnp.float32
BF16 = jnp.bfloat16


def mm(left, right):
    return jnp.dot(left.astype(BF16), right.astype(BF16), preferred_element_type=F32)


def mm_nt(left, right):
    return lax.dot_general(
        left, right, (((1,), (1,)), ((), ())), preferred_element_type=F32
    )


def split(matrix):
    high = matrix.astype(BF16)
    return high, (matrix - high.astype(F32)).astype(BF16)


def mm_split(left, right):
    left_high, left_low = split(left)
    right_high, right_low = split(right)
    return (
        jnp.dot(left_high, right_high, preferred_element_type=F32)
        + jnp.dot(left_high, right_low, preferred_element_type=F32)
        + jnp.dot(left_low, right_high, preferred_element_type=F32)
    )


def unit_rows(matrix):
    return matrix * lax.rsqrt(jnp.sum(matrix * matrix, -1, keepdims=True) + 1e-06)


def spread_blocks(columns, count):
    rows = columns.shape[0]
    first = lax.broadcasted_iota(jnp.int32, (rows, 2 * TILE), 1) < TILE
    return jnp.concatenate(
        [
            jnp.where(first, columns[:, 2 * i : 2 * i + 1], columns[:, 2 * i + 1 : 2 * i + 2])
            for i in range(count // 2)
        ],
        axis=1,
    )


def unit_lower_inverse(lower, row, col):
    size = lower.shape[0]
    inverse = jnp.where(row == col, 1.0, 0.0) - jnp.where((row >> 1) == (col >> 1), lower, 0.0)
    shift = 1
    while (1 << shift) < size:
        corner = ((row >> (shift + 1)) == (col >> (shift + 1))) & ((row >> shift) != (col >> shift))
        inverse = inverse - mm_split(inverse, mm_split(jnp.where(corner, lower, 0.0), inverse))
        shift += 1
    return inverse


def kernel(
    seq_count,
    head_count,
    tokens_ref,
    w_query_ref,
    w_key_ref,
    w_value_ref,
    w_beta_ref,
    w_out_ref,
    mask_query_ref,
    mask_key_ref,
    mask_value_ref,
    mask_out_ref,
    decay_ref,
    gain_ref,
    out_ref,
    w_in,
    w_o,
    tok,
    small,
    rows_in,
    rows_out,
    local_out,
    local_q,
    ab_send,
    ab_recv,
    prefix,
    x_send,
    x_recv,
    s_send,
    s_recv,
    hidden,
    pair_send,
    pair_recv,
    own_part,
    sum_send,
    sum_recv,
    w_sem,
    tok_send_sem,
    tok_recv_sem,
    sib_send_sem,
    sib_recv_sem,
    ab_send_sem,
    ab_recv_sem,
    x_send_sem,
    x_recv_sem,
    s_send_sem,
    s_recv_sem,
    pair_send_sem,
    pair_recv_sem,
    sum_send_sem,
    sum_recv_sem,
):
    s = lax.axis_index("seq")
    hd = lax.axis_index("head")
    chips_x = seq_count // RING
    chips_y = head_count // CORES
    x, z = s // RING, lax.rem(s, RING)
    y, core = hd // CORES, lax.rem(hd, CORES)
    piece, width = tokens_ref.shape
    span = piece * head_count
    key_cols = w_query_ref.shape[1]
    value_cols = w_value_ref.shape[1]
    heads = value_cols // HD
    key_heads = key_cols // HD
    in_cols = 2 * key_cols + value_cols

    weight_copies = [
        pltpu.make_async_copy(w_query_ref, w_in.at[:, pl.ds(0, key_cols)], w_sem.at[0]),
        pltpu.make_async_copy(w_key_ref, w_in.at[:, pl.ds(key_cols, key_cols)], w_sem.at[1]),
        pltpu.make_async_copy(w_value_ref, w_in.at[:, pl.ds(2 * key_cols, value_cols)], w_sem.at[2]),
        pltpu.make_async_copy(w_out_ref, w_o, w_sem.at[3]),
    ]
    for copy in weight_copies:
        copy.start()

    def at_y(step):
        return (s, lax.rem(y + step, chips_y) * CORES + core)

    sibling = (s, y * CORES + (1 - core))

    def at_z(place):
        return (x * RING + place, hd)

    def at_x(step):
        return (lax.rem(x + step, chips_x) * RING + z, hd)

    barrier = pltpu.get_barrier_semaphore()
    partners = [at_y(step) for step in range(1, chips_y)]
    partners += [sibling]
    partners += [at_z(lax.rem(z + step, RING)) for step in range(1, RING)]
    partners += [at_x(step) for step in range(1, chips_x)]
    for partner in partners:
        pl.semaphore_signal(barrier, inc=1, device_id=partner, device_id_type=MESH)
    pl.semaphore_wait(barrier, len(partners))

    def push(source, target, send_sem, recv_sem, device):
        return pltpu.make_async_remote_copy(
            src_ref=source,
            dst_ref=target,
            send_sem=send_sem,
            recv_sem=recv_sem,
            device_id=device,
            device_id_type=MESH,
        )

    far_first = sorted(range(1, chips_y), key=lambda step: -min(step, chips_y - step))
    token_pushes = {
        step: push(
            tokens_ref, tok.at[hd], tok_send_sem.at[step], tok_recv_sem.at[step], at_y(step)
        )
        for step in far_first
    }
    for step in far_first:
        token_pushes[step].start()
    sibling_pushes = [
        push(tokens_ref, tok.at[hd], sib_send_sem.at[0], sib_recv_sem.at[0], sibling)
    ]
    sibling_pushes[0].start()
    tok[hd] = tokens_ref[...]

    small[...] = jnp.zeros_like(small)
    mask_blocks = 0
    for ref in (mask_query_ref, mask_key_ref, mask_value_ref):
        small[mask_blocks : mask_blocks + ref.shape[0], 0 : ref.shape[1]] = ref[...].astype(F32)
        mask_blocks += ref.shape[0]
    turned = jnp.transpose(small[:, 0:HD])
    rows_in[...] = spread_blocks(turned[0 : rows_in.shape[0], :], mask_blocks)
    rows_out[...] = spread_blocks(mask_out_ref[...].astype(F32), mask_out_ref.shape[1])

    for copy in weight_copies[:3]:
        copy.wait()

    def mask_in(i, carry):
        at = pl.ds(pl.multiple_of(i * TILE, TILE), TILE)
        w_in[at, :] = (w_in[at, :].astype(F32) * rows_in[pl.ds(i, 1), :]).astype(BF16)
        return carry

    lax.fori_loop(0, width // TILE, mask_in, 0)

    for step in sorted(range(1, chips_y), key=lambda step: min(step, chips_y - step)):
        token_pushes[step].wait_recv()
        held = tok.at[lax.rem(y + chips_y - step, chips_y) * CORES + core]
        forward = push(held, held, sib_send_sem.at[step], sib_recv_sem.at[step], sibling)
        forward.start()
        sibling_pushes.append(forward)

    weight_copies[3].wait()

    def mask_o(i, carry):
        at = pl.ds(pl.multiple_of(i * TILE, TILE), TILE)
        w_o[at, :] = (w_o[at, :].astype(F32) * rows_out[pl.ds(i, 1), :]).astype(BF16)
        return carry

    lax.fori_loop(0, value_cols // TILE, mask_o, 0)

    row = lax.broadcasted_iota(jnp.int32, (span, span), 0)
    col = lax.broadcasted_iota(jnp.int32, (span, span), 1)
    log_rows = jnp.dot(
        jnp.log(decay_ref[...]),
        jnp.where(row <= col, 1.0, 0.0),
        precision=lax.Precision.HIGHEST,
        preferred_element_type=F32,
    )

    for forward in sibling_pushes:
        forward.wait_recv()

    gathered = tok[...].reshape(span, width)
    beta_rows = jax.nn.sigmoid(mm_nt(w_beta_ref[...], gathered))
    small[0:heads, :] = log_rows
    small[8 : 8 + heads, :] = beta_rows
    columns = jnp.transpose(small[...])

    raw_q = jnp.dot(gathered, w_in[:, 0:key_cols], preferred_element_type=F32)
    raw_k = jnp.dot(gathered, w_in[:, key_cols : 2 * key_cols], preferred_element_type=F32)
    queries, keys, key_turned, grams, pair_scores = [], [], [], [], []
    for i in range(key_heads):
        at = slice(i * HD, (i + 1) * HD)
        query = (unit_rows(raw_q[:, at]) * (1.0 / math.sqrt(HD))).astype(BF16)
        key = unit_rows(raw_k[:, at]).astype(BF16)
        queries.append(query.astype(F32))
        keys.append(key.astype(F32))
        key_turned.append(jnp.transpose(key.astype(F32)))
        grams.append(mm_nt(key, key))
        pair_scores.append(mm_nt(query, key))
    raw_v = jnp.dot(gathered, w_in[:, 2 * key_cols : in_cols], preferred_element_type=F32)
    values = jax.nn.silu(raw_v).astype(BF16).astype(F32)

    eye = jnp.where(
        lax.broadcasted_iota(jnp.int32, (HD, HD), 0) == lax.broadcasted_iota(jnp.int32, (HD, HD), 1),
        1.0,
        0.0,
    )
    is_root = lax.rem(z, CORES) == core
    ab_pushes = []
    for h in range(heads):
        i = h * key_heads // heads
        log_row = log_rows[h : h + 1, :]
        log_col = columns[:, h : h + 1]
        beta_col = columns[:, 8 + h : 9 + h]
        last = log_row[:, span - 1 : span]
        decay = jnp.where(row >= col, jnp.exp(jnp.where(row >= col, log_col - log_row, 0.0)), 0.0)
        lower = jnp.where(row > col, beta_col * decay * grams[i], 0.0)
        inverse = unit_lower_inverse(lower, row, col)
        rise = jnp.exp(log_col)
        value = values[:, h * HD : (h + 1) * HD]
        mixed = mm(
            inverse,
            jnp.concatenate([(beta_col * rise) * keys[i], beta_col * value], axis=1),
        ).astype(BF16)
        tail_keys = key_turned[i] * jnp.exp(last - log_row)
        end = mm(tail_keys, mixed)
        transition = jnp.exp(last) * eye - end[:, 0:HD]
        ab_send[h] = jnp.concatenate([transition, end[:, HD : 2 * HD]], axis=1).astype(BF16)
        target = h * CORES + core
        copy = push(ab_send.at[h], ab_recv.at[z], ab_send_sem.at[h], ab_recv_sem.at[z], at_z(target))
        ab_pushes.append((target, copy))

        @pl.when(z != target)
        def _():
            copy.start()

        @pl.when(z == target)
        def _():
            ab_recv[z] = ab_send[h]

        read = mm(pair_scores[i] * decay, mixed)
        local_out[h] = read[:, HD : 2 * HD]
        local_q[h] = (rise * queries[i] - read[:, 0:HD]).astype(BF16)

    def s_push(place):
        mine = z // CORES
        return push(
            s_send.at[place], s_recv.at[mine], s_send_sem.at[place], s_recv_sem.at[mine], at_z(place)
        )

    def recv_ab(place):
        return push(
            ab_send.at[0], ab_recv.at[place], ab_send_sem.at[0], ab_recv_sem.at[place], at_z(place)
        )

    @pl.when(is_root)
    def _():
        running = None
        for place in range(RING):
            @pl.when(z != place)
            def _():
                recv_ab(place).wait_recv()

            pair = ab_recv[place]
            if place == 0:
                running = pair.astype(F32)
            else:
                running = mm(pair[:, 0:HD], running)
                running = jnp.concatenate(
                    [running[:, 0:HD], running[:, HD : 2 * HD] + pair[:, HD : 2 * HD].astype(F32)], axis=1
                )
            if place < RING - 1:
                prefix[place] = running
        x_send[...] = running.astype(BF16)
        x_pushes = [
            push(x_send, x_recv.at[x], x_send_sem.at[step], x_recv_sem.at[step], at_x(step))
            for step in range(1, chips_x)
        ]
        for copy in x_pushes:
            copy.start()
        x_recv[x] = x_send[...]
        for copy in x_pushes:
            copy.wait_recv()
        state = jnp.zeros((HD, HD), F32)
        for place in range(chips_x - 1):
            pair = x_recv[place]
            after = mm(pair[:, 0:HD], state) + pair[:, HD : 2 * HD].astype(F32)
            state = jnp.where(place < x, after, state)
        for place in range(RING):
            if place == 0:
                start = state
            else:
                start = mm(prefix[place - 1, :, 0:HD], state) + prefix[place - 1, :, HD : 2 * HD]
            s_send[place] = start.astype(BF16)

            @pl.when(z != place)
            def _():
                s_push(place).start()

            @pl.when(z == place)
            def _():
                s_recv[z // CORES] = s_send[place]

        for copy in x_pushes:
            copy.wait_send()
        for place in range(RING):
            @pl.when(z != place)
            def _():
                s_push(place).wait_send()

    for h in range(heads):
        source = h * CORES + core

        @pl.when(z != source)
        def _():
            push(
                s_send.at[0], s_recv.at[h], s_send_sem.at[0], s_recv_sem.at[h], at_z(source)
            ).wait_recv()

        state_out = local_out[h] + jnp.dot(local_q[h], s_recv[h], preferred_element_type=F32)
        inv_rms = lax.rsqrt(jnp.mean(state_out * state_out, -1, keepdims=True) + 1e-06)
        hidden[:, :, h * HD : (h + 1) * HD] = (
            (state_out * inv_rms * gain_ref[...]).astype(BF16).reshape(head_count, piece, HD)
        )

    order = far_first + [0]

    def project(which_core):
        rows = jnp.concatenate(
            [hidden[lax.rem(y + step, chips_y) * CORES + which_core] for step in order], axis=0
        )
        return jnp.dot(rows, w_o[...], preferred_element_type=F32)

    pair_send[...] = project(1 - core).astype(BF16).reshape(chips_y, piece, width)
    pair_pushes = [
        push(pair_send.at[n], pair_recv.at[n], pair_send_sem.at[n], pair_recv_sem.at[n], sibling)
        for n in range(chips_y)
    ]
    for copy in pair_pushes:
        copy.start()
    own_part[...] = project(core).reshape(chips_y, piece, width)
    sum_pushes = []
    for n, step in enumerate(order):
        pair_pushes[n].wait_recv()
        both = own_part[n] + pair_recv[n].astype(F32)
        if step == 0:
            total = both
        else:
            sum_send[n] = both.astype(BF16)
            copy = push(sum_send.at[n], sum_recv.at[n], sum_send_sem.at[n], sum_recv_sem.at[n], at_y(step))
            copy.start()
            sum_pushes.append(copy)
    for n, copy in enumerate(sum_pushes):
        copy.wait_recv()
        total = total + sum_recv[n].astype(F32)
    out_ref[...] = total.astype(BF16)

    for step in far_first:
        token_pushes[step].wait_send()
    for copy in sibling_pushes + pair_pushes + sum_pushes:
        copy.wait_send()
    for target, copy in ab_pushes:
        @pl.when(z != target)
        def _():
            copy.wait_send()


def on_device(
    seq_count,
    head_count,
    tokens,
    w_query,
    w_key,
    w_value,
    w_beta,
    w_out,
    mask_query,
    mask_key,
    mask_value,
    mask_out,
    decay_rate,
    norm_gain,
):
    piece, width = tokens.shape
    span = piece * head_count
    value_cols = w_value.shape[1]
    in_cols = 2 * w_query.shape[1] + value_cols
    heads = value_cols // HD
    chips_x = seq_count // RING
    chips_y = head_count // CORES
    vmem = pl.BlockSpec(memory_space=pltpu.VMEM)
    hbm = pl.BlockSpec(memory_space=pl.ANY)
    dma = pltpu.SemaphoreType.DMA
    return pl.pallas_call(
        functools.partial(kernel, seq_count, head_count),
        out_shape=jax.ShapeDtypeStruct((piece, width), BF16),
        in_specs=[vmem, hbm, hbm, hbm, vmem, hbm] + [vmem] * 6,
        out_specs=vmem,
        scratch_shapes=[
            pltpu.VMEM((width, in_cols), BF16),
            pltpu.VMEM((value_cols, width), BF16),
            pltpu.VMEM((head_count, piece, width), BF16),
            pltpu.VMEM((HD, span), F32),
            pltpu.VMEM((width // TILE, in_cols), F32),
            pltpu.VMEM((value_cols // TILE, width), F32),
            pltpu.VMEM((heads, span, HD), F32),
            pltpu.VMEM((heads, span, HD), BF16),
            pltpu.VMEM((heads, HD, 2 * HD), BF16),
            pltpu.VMEM((RING, HD, 2 * HD), BF16),
            pltpu.VMEM((RING - 1, HD, 2 * HD), F32),
            pltpu.VMEM((HD, 2 * HD), BF16),
            pltpu.VMEM((chips_x, HD, 2 * HD), BF16),
            pltpu.VMEM((RING, HD, HD), BF16),
            pltpu.VMEM((heads, HD, HD), BF16),
            pltpu.VMEM((head_count, piece, value_cols), BF16),
            pltpu.VMEM((chips_y, piece, width), BF16),
            pltpu.VMEM((chips_y, piece, width), BF16),
            pltpu.VMEM((chips_y, piece, width), F32),
            pltpu.VMEM((chips_y - 1, piece, width), BF16),
            pltpu.VMEM((chips_y - 1, piece, width), BF16),
            dma((4,)),
            dma((chips_y,)),
            dma((chips_y,)),
            dma((chips_y,)),
            dma((chips_y,)),
            dma((heads,)),
            dma((RING,)),
            dma((chips_x,)),
            dma((chips_x,)),
            dma((RING,)),
            dma((heads,)),
            dma((chips_y,)),
            dma((chips_y,)),
            dma((chips_y - 1,)),
            dma((chips_y - 1,)),
        ],
        compiler_params=pltpu.CompilerParams(
            collective_id=0, has_side_effects=True, vmem_limit_bytes=48 * 1024 * 1024
        ),
        name="layer",
    )(
        tokens,
        w_query,
        w_key,
        w_value,
        w_beta.T,
        w_out,
        mask_query.T,
        mask_key.T,
        mask_value.T,
        mask_out,
        decay_rate.T,
        norm_gain.reshape(1, HD),
    )


def solution(mesh):
    return jax.shard_map(
        functools.partial(on_device, mesh.shape["seq"], mesh.shape["head"]),
        mesh=mesh,
        in_specs=(
            P(("seq", "head"), None),
            P(None, "head"),
            P(None, "head"),
            P(None, "head"),
            P(None, "head"),
            P("head", None),
            P(None, "head"),
            P(None, "head"),
            P(None, "head"),
            P("head", None),
            P("seq", "head"),
            P(),
        ),
        out_specs=P(("seq", "head"), None),
        check_vma=False,
    )
```

time: 508 us -> 80.3 us (0.16)
  starting transfers between devices: 162 us -> 0 us
  waiting for transfers between devices: 154 us -> 0 us
  other arithmetic: 92.7 us -> 0 us
  Pallas kernels: 0 us -> 69.4 us
  matrix products: 41.5 us -> 0 us
  local copies, waits for them, and re-layouts: 39.4 us -> 10.4 us
  between operations: 14 us -> 0.02 us
    ppermute x31 -> x0, starting transfers between devices: 162 us -> none  [shifted(): return lax.ppermute(block, axis, route)]
    reduce_scatter x1 -> x0, waiting for transfers between devices: 85 us -> none  [on_device(): lax.psum_scatter(jnp.dot(hidden, out_weight, preferred_element_type=jnp.f...]
    another operation x7 -> x0, other arithmetic: 82.3 us -> none  [the longest x5 80.5 us: block_parts(): jax.scipy.linalg.solve_triangular(system, right_side, lower=True, unit_di...]
    pallas_call x0 -> x1, Pallas kernels: none -> 69.4 us  [on_device(): pl.pallas_call(functools.partial(kernel, seq_count, head_count), out_shap...]
    ppermute x31 -> x0, waiting for transfers between devices: 65.2 us -> none  [shifted(): return lax.ppermute(block, axis, route)]
    dot_general x62 -> x0, matrix products: 39.9 us -> none  [the longest x31 12.2 us: hop(): jnp.einsum('hde,hew->hdw', transition, incoming, precision=highest) + offset]
    convert_element_type x10 -> x0, local copies, waits for them, and re-layouts: 18.1 us -> none  [the longest x7 17.1 us: masked(): return weight * full.astype(weight.dtype)]
    unnamed x54 -> x23, local copies, waits for them, and re-layouts: 1.46 us -> 10.4 us
  transfers between devices with their start and end apart: 33 -> 0, of which waited for: 33 -> 0; matrix products, arithmetic and copies ran while one was open for 6% -> 0% of each run, Pallas kernels for 0% -> 0%
where the time goes in v1:
time: 80.3 us; the launch traced here: 79.8 us
  Pallas kernels  69.4 us (86%)
  local copies, waits for them, and re-layouts  10.4 us (13%)
    pallas_call x1, Pallas kernels, on_device(): pl.pallas_call(functools.partial(kernel, seq_count, head_count), out_shap...  69.4 us
    unnamed x23, local copies, waits for them, and re-layouts  10.4 us

profile of v1, /device:TPU:1, one launch (start us, length us, event | category | flops | bytes accessed | tf_op | source)
XLA Modules:
  0.0 79.8 jit_solution(7839630279623655499)
XLA Ops:
  0.0 0.0 copy-start
  0.0 1.6 %copy-done = bf16[2048,512]{1,0:T(8,128)(2,1)S(1)} copy-done((bf16[2048,512]{1,0:T(8,128)(2,1)S(1)}, bf16[2048,512]{1,0:T(8,128)(2,1)}, u32[]{:S(2)}) %copy-start) | copy-done | bytes 2097176
  1.6 0.0 copy-start.1
  1.6 1.2 %copy-done.1 = bf16[2048,256]{1,0:T(8,128)(2,1)S(1)} copy-done((bf16[2048,256]{1,0:T(8,128)(2,1)S(1)}, bf16[2048,256]{1,0:T(8,128)(2,1)}, u32[]{:S(2)}) %copy-start.1) | copy-done | bytes 1048600
  2.8 0.0 copy-start.2
  2.8 1.2 %copy-done.2 = bf16[2048,256]{1,0:T(8,128)(2,1)S(1)} copy-done((bf16[2048,256]{1,0:T(8,128)(2,1)S(1)}, bf16[2048,256]{1,0:T(8,128)(2,1)}, u32[]{:S(2)}) %copy-start.2) | copy-done | bytes 1048600
  4.0 0.0 copy-start.3
  4.0 0.9 %copy-done.3 = bf16[32,2048]{1,0:T(8,128)(2,1)S(1)} copy-done((bf16[32,2048]{1,0:T(8,128)(2,1)S(1)}, bf16[32,2048]{1,0:T(8,128)(2,1)}, u32[]{:S(2)}) %copy-start.3) | copy-done | bytes 131096
  4.9 0.0 copy-start.4
  4.9 0.7 copy-done.4
  5.7 0.0 copy-start.5
  5.7 0.7 copy-done.5
  6.4 0.0 copy-start.6
  6.4 0.7 copy-done.6
  7.0 0.0 copy-start.7
  7.0 0.7 copy-done.7
  7.7 0.0 copy-start.8
  7.7 0.7 copy-done.8
  8.4 0.0 copy-start.9
  8.4 0.7 copy-done.9
  9.1 0.0 copy-start.10
  9.1 0.7 copy-done.10
  9.7 69.4 %layer.1 = bf16[32,2048]{1,0:T(8,128)(2,1)S(1)} custom-call(bf16[32,2048]{1,0:T(8,128)(2,1)S(1)} %copy-done.3, bf16[2048,256]{1,0:T(8,128)(2,1)S(1)} %copy-done.1, bf16[2048,256]{1,0:T(8,128)(2,1)S(1)} %copy-done.2, bf16[2048,512]{1,0:T(8,128)(2,1)S(1)} %copy-done, bf16[4,2048]{1,0:T(4,128)(2,1)S(1)} %bitcast.6, bf16[512,2048]{1,0:T(8,128)(2,1)} %w_out_ref.1, ...), custom_call_target="tpu_custom_call" | custom-call | tf_op jit(solution)/shard_map/layer/pallas_call | solution.py:452
  79.2 0.7 copy.14
Async XLA Ops:
  0.0 1.6 %copy-start = (bf16[2048,512]{1,0:T(8,128)(2,1)S(1)}, bf16[2048,512]{1,0:T(8,128)(2,1)}, u32[]{:S(2)}) copy-start(bf16[2048,512]{1,0:T(8,128)(2,1)} %w_value_ref.1) | copy-start | bytes 6291460
  1.6 1.2 %copy-start.1 = (bf16[2048,256]{1,0:T(8,128)(2,1)S(1)}, bf16[2048,256]{1,0:T(8,128)(2,1)}, u32[]{:S(2)}) copy-start(bf16[2048,256]{1,0:T(8,128)(2,1)} %w_query_ref.1) | copy-start | bytes 3145732
  2.8 1.2 %copy-start.2 = (bf16[2048,256]{1,0:T(8,128)(2,1)S(1)}, bf16[2048,256]{1,0:T(8,128)(2,1)}, u32[]{:S(2)}) copy-start(bf16[2048,256]{1,0:T(8,128)(2,1)} %w_key_ref.1) | copy-start | bytes 3145732
  4.0 0.9 %copy-start.3 = (bf16[32,2048]{1,0:T(8,128)(2,1)S(1)}, bf16[32,2048]{1,0:T(8,128)(2,1)}, u32[]{:S(2)}) copy-start(bf16[32,2048]{1,0:T(8,128)(2,1)} %tokens_ref.1) | copy-start | bytes 393220
  4.9 0.7 copy-start.4
  5.7 0.7 copy-start.5
  6.4 0.7 copy-start.6
  7.0 0.7 copy-start.7
  7.7 0.7 copy-start.8
  8.4 0.7 copy-start.9
  9.1 0.7 copy-start.10
